TPU v7x, 128 devices: a whole 4x4x4 slice. The times are simulated.
128 devices in a mesh: seq: 8 (over y, x_hi), chan: 16 (over x_lo, z, core).
Axes of the slice: x: 4 (x_hi: 2, x_lo: 2; x = x_hi * 2 + x_lo), y: 4, z: 4, core: 2. Of those that a mesh axis runs over, the one named last changes fastest.
Arguments:
- query_rows: bfloat16 [8192, 8192], P('seq', 'chan'), may hold values from -6 to 6
- key_rows: bfloat16 [8192, 8192], P('seq', 'chan'), may hold values from -6 to 6
- value_rows: bfloat16 [8192, 8192], P('seq', 'chan'), may hold values from -6 to 6
- horizon: float32 [16, 8192], P(None, 'chan'), may hold values from 30 to 32768
- residue: float32 [16, 8192], P(None, 'chan'), may hold values from -1.5 to 1.5
- skip: float32 [8192], P('chan'), may hold values from -4 to 4
- w_out: bfloat16 [8192, 8192], P('chan'), may hold values from -0.09375 to 0.09375
Outputs:
- output: bfloat16 [8192, 8192], P('seq', 'chan')
All inputs are finite; a program needn't handle non-finite values.
Results may differ from a plain program's by a relative error of at most 0.0049.
Values may be sent and summed in bfloat16 or wider, within the bound.
A program may use at most 192 MiB of HBM per device.

v0:
```python
import jax
import jax.numpy as jnp
from jax import lax
from jax.sharding import PartitionSpec as P


def entering(value, axis, join, neutral):
    count, mine = (lax.axis_size(axis), lax.axis_index(axis))
    pieces = jax.tree.map(lambda part: lax.all_gather(part, axis), value)
    subtotal = jax.tree.map(
        lambda part, zero: jnp.full_like(part, 0) + jnp.asarray(zero, part.dtype), value, neutral
    )

    def hop(position, subtotal):
        longer = join(subtotal, jax.tree.map(lambda part: part[position], pieces))
        return jax.tree.map(lambda new, old: jnp.where(position < mine, new, old), longer, subtotal)

    return lax.fori_loop(0, count - 1, hop, subtotal)


def join_states(earlier, later):
    return (earlier[0] * later[0], later[0] * earlier[1] + later[1])


def local(query_rows, key_rows, value_rows, horizon, residue, skip, w_out):
    seq_rows, chan_width = query_rows.shape
    block_len = min(128, seq_rows)
    block_count = seq_rows // block_len
    rate = 1.0 / horizon
    scaled = residue * jnp.sqrt(-jnp.expm1(-2.0 * rate))
    mixed = key_rows.astype(jnp.float32) * value_rows.astype(jnp.float32)
    pieces = mixed.reshape(block_count, block_len, chan_width)
    step_index = jnp.arange(block_len, dtype=jnp.int32)
    offsets = step_index.astype(jnp.float32)
    powers = jnp.exp(-rate[:, None, :] * offsets[None, :, None])
    kernel = jnp.sum(powers * scaled[:, None, :], axis=0)
    lags = step_index[:, None] - step_index[None, :]
    toeplitz = jnp.where(
        (lags >= 0)[:, :, None], jnp.take(kernel, jnp.maximum(lags, 0), axis=0), 0.0
    )
    inner = jnp.einsum("tsc,nsc->ntc", toeplitz, pieces, precision=lax.Precision.HIGHEST)
    local_end = jnp.einsum(
        "msc,nsc->nmc", powers[:, ::-1, :], pieces, precision=lax.Precision.HIGHEST
    )
    order = jnp.arange(block_count, dtype=jnp.int32)
    gaps = order[:, None] - 1 - order[None, :]
    spans = jnp.maximum(gaps, 0).astype(jnp.float32)
    carry_mat = jnp.where(
        (gaps >= 0)[:, :, None, None],
        jnp.exp(-rate[None, None] * (block_len * spans)[:, :, None, None]),
        0.0,
    )
    before_local = jnp.einsum(
        "njmc,jmc->nmc", carry_mat, local_end, precision=lax.Precision.HIGHEST
    )
    device_end = jnp.exp(-rate * block_len) * before_local[-1] + local_end[-1]
    device_decay = jnp.exp(-rate * seq_rows)
    identity = (jnp.ones_like(rate), jnp.zeros_like(rate))
    incoming = entering((device_decay, device_end), "seq", join_states, identity)[1]
    starts = order.astype(jnp.float32) * block_len
    before = before_local + jnp.exp(-rate[None] * starts[:, None, None]) * incoming[None]
    lead = powers * (scaled * jnp.exp(-rate))[:, None, :]
    outer = jnp.einsum("mtc,nmc->ntc", lead, before, precision=lax.Precision.HIGHEST)
    conv = (inner + outer).reshape(seq_rows, chan_width)
    gated = (query_rows.astype(jnp.float32) * (conv + skip[None, :] * mixed)).astype(jnp.bfloat16)
    shares = lax.psum_scatter(
        lax.dot_general(w_out, gated, (((0,), (1,)), ((), ())), preferred_element_type=jnp.float32),
        "chan",
        scatter_dimension=0,
        tiled=True,
    )
    output = shares.T.astype(jnp.bfloat16)
    return output


def solution(mesh):
    in_specs = (
        P("seq", "chan"),
        P("seq", "chan"),
        P("seq", "chan"),
        P(None, "chan"),
        P(None, "chan"),
        P("chan"),
        P("chan", None),
    )
    out_specs = P("seq", "chan")
    return jax.shard_map(local, mesh=mesh, in_specs=in_specs, out_specs=out_specs, check_vma=False)
```

profile of v0, /device:TPU:1, one launch (start us, length us, event | category | flops | bytes accessed | tf_op | source)
XLA Modules:
  0.0 509.5 jit_solution(14333995060702796019)
XLA Ops:
  6.8 0.8 exponential_multiply_fusion
  7.9 7.6 %multiply_exponential_fusion = (f32[16,128,512]{1,0,2:T(8,128)}, f32[128,512]{0,1:T(8,128)}) fusion(f32[128]{0:T(128)S(1)} %iota_convert_fusion, f32[16,512]{0,1:T(8,128)S(1)} %copy.42, f32[16,512]{0,1:T(8,128)S(1)} %copy.43), kind=kLoop, calls=%fused_computation.15 | loop fusion | flops 3080192 | bytes 4522496 | tf_op jit(solution)/shard_map/exp | solution.py:35
  15.5 7.3 %rev.3 = f32[16,128,512]{1,0,2:T(8,128)} reverse(f32[16,128,512]{1,0,2:T(8,128)} %get-tuple-element.135), dimensions={1} | reverse | bytes 8388608 | tf_op jit(solution)/shard_map/rev | solution.py:43
  22.8 1.6 convert_multiply_fusion
  24.5 2.1 copy.46
  26.6 9.4 %fusion.24 = f32[512,8,16]{2,1,0:T(8,128)} fusion(f32[8,128,512]{1,0,2:T(8,128)S(1)} %copy.46, f32[16,128,512]{1,0,2:T(8,128)} %rev.3), kind=kOutput, calls=%fused_computation.48 | convolution fusion | flops 100663296 | bytes 6553600 | tf_op jit(solution)/shard_map/msc,nsc->nmc/dot_general | solution.py:42
  35.9 2.9 copy.48
  38.8 2.9 copy.62
  41.7 1.5 multiply_reduce_fusion.1
  44.7 31.6 %all-gather.1 = f32[128,512]{1,0:T(8,128)} all-gather(f32[16,512]{1,0:T(8,128)S(1)} %get-tuple-element.137), channel_id=3, replica_groups=mesh['seq'=8,'chan'=16] {'seq'}, dimensions={0}, use_global_device_ids=true | all-gather | bytes 294912 | tf_op jit(solution)/shard_map/all_gather | solution.py:9
  76.3 31.5 %all-gather = f32[128,512]{1,0:T(8,128)} all-gather(f32[16,512]{1,0:T(8,128)S(1)} %get-tuple-element.138), channel_id=2, replica_groups=mesh['seq'=8,'chan'=16] {'seq'}, dimensions={0}, use_global_device_ids=true | all-gather | bytes 294912 | tf_op jit(solution)/shard_map/all_gather | solution.py:9
  107.9 5.7 %while.14 = (s32[]{:T(128)}, f32[16,512]{1,0:T(8,128)S(1)}, s32[]{:T(128)}, f32[8,16,512]{2,1,0:T(8,128)}, f32[8,16,512]{2,1,0:T(8,128)}, /*index=5*/s32[]{:T(128)}, s32[]{:T(128)}) while((s32[]{:T(128)}, f32[16,512]{1,0:T(8,128)S(1)}, s32[]{:T(128)}, f32[8,16,512]{2,1,0:T(8,128)}, f32[8,16,512]{2,1,0:T(8,128)}, ...), condition=%wide.region_2.3_spmd.clone, body=%wide.region_1.2_spmd.clone.sunk | while | flops 32772 | bytes 131173 | solution.py:18
  107.9 0.8 fusion.35
  108.7 0.8 fusion.35
  109.5 0.8 fusion.35
  110.3 0.8 fusion.35
  111.1 0.8 fusion.35
  111.9 0.8 fusion.35
  112.7 0.8 fusion.35
  113.5 1.8 multiply_add_fusion
  115.3 2.9 copy.50
  118.2 1.1 copy.44
  119.3 64.3 %gather_fusion = f32[16384,512]{1,0:T(8,128)} fusion(f32[128,512]{1,0:T(8,128)S(1)} %copy.44, s32[16384]{0:T(1024)S(1)} %bitcast_clamp_fusion), kind=kCustom, calls=%fused_computation | custom fusion | bytes 67174400 | tf_op jit(solution)/shard_map/jit(_take)/gather | solution.py:39
  183.6 35.6 %copy.45 = f32[128,128,512]{1,0,2:T(8,128)} copy(f32[128,128,512]{2,1,0:T(8,128)} %bitcast.55) | data formatting | bytes 67108864 | tf_op jit(solution)/shard_map/jit(_take)/gather | solution.py:39
  219.1 0.8 copy.49
  220.0 55.9 %fusion.1 = f32[512,8,128]{2,1,0:T(8,128)S(1)} fusion(f32[8,128,512]{1,0,2:T(8,128)S(1)} %copy.46, f32[128,128,512]{1,0,2:T(8,128)} %copy.45, pred[128,128]{1,0:T(8,128)(4,1)S(1)} %get-tuple-element.140, pred[128,128]{1,0:T(8,128)(4,1)S(1)} %get-tuple-element.141), kind=kOutput, calls=%fused_computation.4 | convolution fusion | flops 822083584 | bytes 37781504 | tf_op jit(solution)/shard_map/tsc,nsc->ntc/dot_general | solution.py:41
  276.0 6.8 %add_bitcast_fusion = f32[8,128,512]{1,0,2:T(8,128)} fusion(f32[512,8,128]{2,1,0:T(8,128)S(1)} %fusion.1, f32[8,16,512]{1,0,2:T(8,128)S(1)} %copy-done.2, f32[16,512]{0,1:T(8,128)S(1)} %copy-done.6, f32[128]{0:T(128)S(1)} %iota_convert_fusion, f32[16,512]{0,1:T(8,128)S(1)} %copy-done.4), kind=kOutput, calls=%fused_computation.20 | convolution fusion | flops 103284736 | bytes 4522496 | tf_op jit(solution)/shard_map/mtc,nmc->ntc/dot_general | solution.py:63
  282.7 1.9 copy.61
  284.7 2.3 fusion.11
  287.0 17.9 %convolution_bitcast_fusion = f32[8192,1024]{0,1:T(8,128)} fusion(bf16[1024,512]{1,0:T(8,128)(2,1)S(1)} %fusion.11, bf16[512,8192]{1,0:T(8,128)(2,1)} %param.15), kind=kOutput, calls=%fused_computation.7 | convolution fusion | flops 8589934592 | bytes 42991616 | tf_op jit(solution)/shard_map/dot_general | solution.py:67
  304.9 195.1 %reduce-scatter.2.cloned.1.call-done = f32[512,1024]{0,1:T(8,128)} async-done(((f32[8192,1024]{0,1:T(8,128)}), f32[512,1024]{0,1:T(8,128)}) %reduce-scatter.2.cloned.1.call-update) | async-done | bytes 2097168 | tf_op jit(solution)/shard_map/reduce_scatter | solution.py:66
  500.0 2.7 convert_bitcast_fusion
  (31 shorter events, 2.0 us)
Async XLA Ops:
  6.5 493.5 %reduce-scatter.2.cloned.1.call-start = ((), (), s32[]{:S(2)}) async-start(), calls=%async_computation.1 | async-start | bytes 35651584 | tf_op jit(solution)/shard_map/reduce_scatter | solution.py:66
  7.7 7.8 %copy-start.3 = (f32[16,512]{0,1:T(8,128)}, f32[16,512]{0,1:T(8,128)S(1)}, u32[]{:S(2)}) copy-start(f32[16,512]{0,1:T(8,128)S(1)} %copy.42) | copy-start | bytes 98308
  15.5 7.3 %copy-start = (bf16[1024,512]{1,0:T(8,128)(2,1)S(1)}, bf16[1024,512]{1,0:T(8,128)(2,1)}, u32[]{:S(2)}) copy-start(bf16[1024,512]{1,0:T(8,128)(2,1)} %param.11) | copy-start | bytes 3145732
  15.5 7.3 %copy-start.1 = (bf16[1024,512]{1,0:T(8,128)(2,1)S(1)}, bf16[1024,512]{1,0:T(8,128)(2,1)}, u32[]{:S(2)}) copy-start(bf16[1024,512]{1,0:T(8,128)(2,1)} %param.10) | copy-start | bytes 3145732
  38.8 5.1 %copy-start.7 = (f32[16,512]{1,0:T(8,128)S(1)}, f32[16,512]{1,0:T(8,128)}, u32[]{:S(2)}) copy-start(f32[16,512]{1,0:T(8,128)} %param.12) | copy-start | bytes 98308
  43.2 0.7 copy-start.5
  220.0 56.0 %copy-start.2 = (f32[8,16,512]{1,0,2:T(8,128)S(1)}, f32[8,16,512]{1,0,2:T(8,128)}, u32[]{:S(2)}) copy-start(f32[8,16,512]{1,0,2:T(8,128)} %copy.50) | copy-start | bytes 786436
  220.0 56.0 %copy-start.4 = (f32[16,512]{0,1:T(8,128)S(1)}, f32[16,512]{0,1:T(8,128)}, u32[]{:S(2)}) copy-start(f32[16,512]{0,1:T(8,128)} %copy-done.3) | copy-start | bytes 98308
  220.0 56.0 %copy-start.6 = (f32[16,512]{0,1:T(8,128)S(1)}, f32[16,512]{0,1:T(8,128)}, u32[]{:S(2)}) copy-start(f32[16,512]{0,1:T(8,128)} %copy.49) | copy-start | bytes 98308
  282.7 2.0 copy-start.8
Sparse Core Ops, SparseCore 0:
  305.0 194.9 reduce-scatter.1
where the time goes:
time: 512 us; the launch traced here: 510 us
  waiting for transfers between devices  195 us (38%)
  local copies, waits for them, and re-layouts  123 us (24%)
  matrix products  89.9 us (18%)
  blocking collectives  63.1 us (12%)
  other arithmetic  24.9 us (5%)
  between operations  13.5 us (3%)
    reduce_scatter x1, waiting for transfers between devices, local(): lax.psum_scatter(lax.dot_general(w_out, gated, (((0,), (1,)), ((), ())),...  195 us
    gather x2, local copies, waits for them, and re-layouts, local(): jnp.take(kernel, jnp.maximum(lags, 0), axis=0)  99.9 us
    all_gather x2, blocking collectives, entering(): pieces = jax.tree.map(lambda part: lax.all_gather(part, axis), value)  63.1 us
    dot_general x1, matrix products, local(): jnp.einsum('tsc,nsc->ntc', toeplitz, pieces, precision=lax.Precision.HIGH...  55.9 us
    dot_general x1, matrix products, local(): lax.dot_general(w_out, gated, (((0,), (1,)), ((), ())), preferred_element...  17.9 us
  transfers between devices with their start and end apart: 1, of which 1 were waited for; matrix products, arithmetic and copies ran while one was open for 0% of the time, Pallas kernels for 0%

commit v1 on v0

v1 whole, which is shorter than its diff:
```python
import functools

import jax
import jax.numpy as jnp
from jax import lax
from jax.experimental import pallas as pl
from jax.experimental.pallas import tpu as pltpu
from jax.sharding import PartitionSpec as P

MESH = pl.DeviceIdType.MESH
F32 = jnp.float32
BF16 = jnp.bfloat16

ROWS = 1024
WIDTH = 512
MODES = 16
SUB = 8
BLOCK = ROWS // SUB
LANES = 128
TILES = WIDTH // LANES
CHUNKS = 8
CHUNK = ROWS // CHUNKS
LAG2 = 2
LAG3 = 4
VIA = {2: (0, 1), 1: (0, 1), 3: (0, 1), 0: (1, 1)}
ORDER = (2, 1, 3, 0)


def place(y, xh, xl, z, core):
    return {"seq": y * 2 + xh, "chan": xl * 8 + z * 2 + core}


def kernel(
    q_hbm, k_hbm, v_hbm, horizon_ref, residue_ref, skip_ref, w_hbm, out_ref,
    stage, mix, gate, decay, coef, skips, local, begin, ends, gat, wn,
    first_out, first_in, second_out, second_in, total,
    stage_sem, wl, wc_s, wc_r, wx_s, wx_r, wy_s, wy_r, st_s, st_r,
    gc_s, gc_r, gx_s, gx_r, gf_s, gf_r, f_s, f_r, s_s, s_r,
):
    seq = lax.axis_index("seq")
    chan = lax.axis_index("chan")
    y, xh = seq // 2, lax.rem(seq, 2)
    xl, z, core = chan // 8, lax.rem(chan // 2, 4), lax.rem(chan, 2)
    parity = lax.rem(y, 2)

    def later(k):
        return {"seq": lax.rem(seq + k, 8), "chan": chan}

    def x_side(hi, c):
        other = lax.rem(core + c, 2)
        return place(y, (1 - xh) if hi else xh, 1 - xl, z, other)

    mate = place(y, xh, xl, z, 1 - core)
    z_up = place(y, xh, xl, lax.rem(z + 1, 4), core)
    z_down = place(y, xh, xl, lax.rem(z + 3, 4), core)
    y_up = place(lax.rem(y + 1, 4), xh, xl, z, core)
    y_down = place(lax.rem(y + 3, 4), xh, xl, z, core)

    barrier = pltpu.get_barrier_semaphore()
    peers = [later(k) for k in range(1, 8)]
    peers += [mate, z_up, z_down]
    peers += [x_side(hi, c) for hi in (0, 1) for c in (0, 1)]
    for peer in peers:
        pl.semaphore_signal(barrier, inc=1, device_id=peer, device_id_type=MESH)

    loads = [
        pltpu.make_async_copy(src, stage.at[i], stage_sem.at[i])
        for i, src in enumerate((k_hbm, v_hbm, q_hbm))
    ]
    for load in loads:
        load.start()

    def remote(src, dst, send, recv, device):
        return pltpu.make_async_remote_copy(
            src_ref=src, dst_ref=dst, send_sem=send, recv_sem=recv,
            device_id=device, device_id_type=MESH,
        )

    def columns(a, d, b):
        block = a * 8 + lax.rem(z + d, 4) * 2 + b
        return pl.ds(pl.multiple_of(block * WIDTH, WIDTH), WIDTH)

    half = WIDTH // 2

    def half_rows(c, p):
        return pl.ds(pl.multiple_of((2 + c) * WIDTH + p * half, half), half)

    def w_x(d, c):
        return remote(
            w_hbm.at[pl.ds(pl.multiple_of(parity * half, half), half),
                     columns(1 - xl, d, lax.rem(core + c, 2))],
            wn.at[d, half_rows(c, parity)],
            wx_s.at[d, c], wx_r.at[d, c], x_side(VIA[d][c], c),
        )

    def w_y(d, c):
        piece = wn.at[d, half_rows(c, parity)]
        return remote(piece, piece, wy_s.at[d, c], wy_r.at[d, c], y_up if c else y_down)

    def w_mate(d):
        return remote(
            w_hbm.at[:, columns(xl, d, 1 - core)],
            wn.at[d, pl.ds(WIDTH, WIDTH)],
            wc_s.at[d], wc_r.at[d], mate,
        )

    def w_own(d):
        return pltpu.make_async_copy(
            w_hbm.at[:, columns(xl, d, core)], wn.at[d, pl.ds(0, WIDTH)], wl.at[d]
        )

    pl.semaphore_wait(barrier, len(peers))
    for d in ORDER:
        for c in (0, 1):
            w_x(d, c).start()
    for d in ORDER:
        w_mate(d).start()
    for d in ORDER:
        w_own(d).start()

    rate = 1.0 / horizon_ref[...]
    twice = 2.0 * rate
    series = jnp.ones_like(twice)
    for n in range(13, 1, -1):
        series = 1.0 - (twice * (1.0 / n)) * series
    power = jnp.where(twice < 0.5, twice * series, 1.0 - jnp.exp(-twice))
    scaled = residue_ref[...] * jnp.sqrt(power)
    step_decay = jnp.exp(-rate)
    block_decay = jnp.exp(-rate * BLOCK)
    device_decay = jnp.exp(-rate * ROWS)
    for t in range(TILES):
        lane = slice(t * LANES, (t + 1) * LANES)
        for m in range(MODES):
            rows = slice(m * SUB, (m + 1) * SUB)
            decay[t, rows, :] = jnp.broadcast_to(step_decay[m:m + 1, lane], (SUB, LANES))
            coef[t, rows, :] = jnp.broadcast_to(scaled[m:m + 1, lane], (SUB, LANES))
        skips[t, :, :] = jnp.broadcast_to(skip_ref[:, lane], (SUB, LANES))

    loads[0].wait()
    loads[1].wait()
    for t in range(TILES):
        lane = pl.ds(t * LANES, LANES)
        for n in range(SUB):
            rows = pl.ds(n * BLOCK, BLOCK)
            mix[t, pl.ds(n, BLOCK, stride=SUB), :] = (
                stage[0, rows, lane].astype(F32) * stage[1, rows, lane].astype(F32)
            )

    def states(ref, t):
        return [ref[t, m * SUB:(m + 1) * SUB, :] for m in range(MODES)]

    def scan_tile(t, carry):
        a = states(decay, t)

        def step(i, h):
            h = list(h)
            for u in range(4):
                x = mix[t, pl.ds(pl.multiple_of((i * 4 + u) * SUB, SUB), SUB), :]
                h = [a[m] * h[m] + x for m in range(MODES)]
            return tuple(h)

        zero = tuple(jnp.zeros((SUB, LANES), F32) for _ in range(MODES))
        h = lax.fori_loop(0, BLOCK // 4, step, zero)
        for m in range(MODES):
            local[t, m * SUB:(m + 1) * SUB, :] = h[m]
        return carry

    lax.fori_loop(0, TILES, scan_tile, 0)

    for t in range(TILES):
        lane = slice(t * LANES, (t + 1) * LANES)
        state = jnp.zeros((MODES, LANES), F32)
        for n in range(SUB):
            begin[t, pl.ds(n, MODES, stride=SUB), :] = state
            state = block_decay[:, lane] * state + local[t, pl.ds(n, MODES, stride=SUB), :]
        ends[0, :, lane] = state

    def state_copy(k):
        return remote(ends.at[0], ends.at[k], st_s.at[k], st_r.at[k], later(k))

    for k in range(1, 8):
        state_copy(k).start()

    loads[2].wait()
    for t in range(TILES):
        lane = pl.ds(t * LANES, LANES)
        for n in range(SUB):
            gate[t, pl.ds(n, BLOCK, stride=SUB), :] = (
                stage[2, pl.ds(n * BLOCK, BLOCK), lane].astype(F32)
            )

    def pass_on(d):
        for c in (0, 1):
            w_x(d, c).wait_recv()
            w_y(d, c).start()

    for k in range(1, 8):
        state_copy(k).wait_recv()
    incoming = jnp.zeros((MODES, WIDTH), F32)
    for k in range(7, 0, -1):
        incoming = jnp.where(k <= seq, device_decay * incoming + ends[k], incoming)
    for n in range(SUB):
        carried = jnp.exp(-rate * (BLOCK * n)) * incoming
        for t in range(TILES):
            rows = pl.ds(n, MODES, stride=SUB)
            begin[t, rows, :] = begin[t, rows, :] + carried[:, t * LANES:(t + 1) * LANES]

    def chunk_rows(r):
        return pl.ds(pl.multiple_of(r * CHUNK, CHUNK), CHUNK)

    def slot(s):
        return pl.ds(s * WIDTH, WIDTH)

    def g_mate(r):
        return remote(
            gat.at[chunk_rows(r), slot(0)], gat.at[chunk_rows(r), slot(1)],
            gc_s.at[r], gc_r.at[r], mate,
        )

    def g_x(r):
        return remote(
            gat.at[chunk_rows(r), slot(0)], gat.at[chunk_rows(r), slot(2)],
            gx_s.at[r], gx_r.at[r], x_side(0, 0),
        )

    def g_pass(r):
        return remote(
            gat.at[chunk_rows(r), slot(2)], gat.at[chunk_rows(r), slot(3)],
            gf_s.at[r], gf_r.at[r], mate,
        )

    def filter_tile(r, t):
        a = states(decay, t)
        b = states(coef, t)
        direct = skips[t, :, :]

        def step(i, h):
            h = list(h)
            parts = []
            base = r * CHUNK + i * (2 * SUB)
            for u in range(2):
                rows = pl.ds(pl.multiple_of(base + u * SUB, SUB), SUB)
                x = mix[t, rows, :]
                h = [a[m] * h[m] + x for m in range(MODES)]
                terms = [b[m] * h[m] for m in range(MODES)]
                while len(terms) > 1:
                    terms = [terms[j] + terms[j + 1] for j in range(0, len(terms), 2)]
                parts.append(gate[t, rows, :] * (terms[0] + direct * x))
            gat[
                pl.ds(pl.multiple_of(base, 2 * SUB), 2 * SUB),
                pl.ds(pl.multiple_of(t * LANES, LANES), LANES),
            ] = jnp.concatenate(parts, axis=0).astype(BF16)
            return tuple(h)

        h = lax.fori_loop(0, CHUNK // (2 * SUB), step, tuple(states(begin, t)))
        for m in range(MODES):
            begin[t, m * SUB:(m + 1) * SUB, :] = h[m]

    def filter_chunk(r, carry):
        def tile(t, carry):
            filter_tile(r, t)
            return carry

        lax.fori_loop(0, TILES, tile, 0)
        g_x(r).start()
        g_mate(r).start()
        return carry

    lax.fori_loop(0, CHUNKS, filter_chunk, 0)
    pass_on(2)
    pass_on(1)

    def w_ready(d):
        for c in (0, 1):
            w_y(d, c).wait_recv()
        w_mate(d).wait_recv()
        w_own(d).wait()

    def product(r, d):
        return jnp.dot(gat[chunk_rows(r), :], wn[d], preferred_element_type=F32)

    def first_copy(r, side):
        part = pl.ds(side * half, half)
        return remote(
            first_out.at[chunk_rows(r), part], first_in.at[chunk_rows(r), part],
            f_s.at[side, r], f_r.at[side, r], z_down if side else z_up,
        )

    def second_copy(r, side):
        return remote(
            second_out.at[side, chunk_rows(r)], second_in.at[side, chunk_rows(r)],
            s_s.at[side, r], s_r.at[side, r], z_down if side else z_up,
        )

    def first_sum(r):
        g_x(r).wait_recv()
        g_pass(r).start()
        g_mate(r).wait_recv()
        g_pass(r).wait_recv()
        first_out[chunk_rows(r), :] = product(r, 2).astype(BF16)
        for side in (0, 1):
            first_copy(r, side).start()

    def second_sum(r):
        for side in (0, 1):
            part = pl.ds(side * half, half)
            rest = pl.ds((1 - side) * half, half)
            partial = product(r, 3 if side else 1)
            first_copy(r, side).wait_recv()
            summed = partial[:, side * half:(side + 1) * half] + first_in[chunk_rows(r), part].astype(F32)
            second_out[side, chunk_rows(r), part] = summed.astype(BF16)
            second_out[side, chunk_rows(r), rest] = partial[:, (1 - side) * half:(2 - side) * half].astype(BF16)
            second_copy(r, side).start()

    def last_sum(r):
        own = product(r, 0)
        for side in (0, 1):
            second_copy(r, side).wait_recv()
        own = own + second_in[0, chunk_rows(r), :].astype(F32) + second_in[1, chunk_rows(r), :].astype(F32)
        for t in range(TILES):
            total[t, :, :] = own[:, t * LANES:(t + 1) * LANES]
        piece = CHUNK // SUB
        for n in range(SUB):
            rows = pl.ds(pl.multiple_of(n * BLOCK + r * piece, piece), piece)
            for t in range(TILES):
                out_ref[rows, t * LANES:(t + 1) * LANES] = (
                    total[t, pl.ds(n, piece, stride=SUB), :].astype(BF16)
                )

    def turn(i, carry):
        @pl.when(i == 0)
        def _():
            w_ready(2)

        @pl.when(i < CHUNKS)
        def _():
            first_sum(i)

        @pl.when(i == LAG2 - 1)
        def _():
            pass_on(3)

        @pl.when(i == LAG2)
        def _():
            w_ready(1)
            w_ready(3)

        @pl.when((i >= LAG2) & (i < CHUNKS + LAG2))
        def _():
            second_sum(i - LAG2)

        @pl.when(i == LAG3 - 1)
        def _():
            pass_on(0)

        @pl.when(i == LAG3)
        def _():
            w_ready(0)

        @pl.when(i >= LAG3)
        def _():
            last_sum(i - LAG3)

        return carry

    lax.fori_loop(0, CHUNKS + LAG3, turn, 0)

    for d in ORDER:
        for c in (0, 1):
            w_x(d, c).wait_send()
            w_y(d, c).wait_send()
        w_mate(d).wait_send()
    for k in range(1, 8):
        state_copy(k).wait_send()

    def finish(r, carry):
        g_x(r).wait_send()
        g_mate(r).wait_send()
        g_pass(r).wait_send()
        for side in (0, 1):
            first_copy(r, side).wait_send()
            second_copy(r, side).wait_send()
        return carry

    lax.fori_loop(0, CHUNKS, finish, 0)


def local(query_rows, key_rows, value_rows, horizon, residue, skip, w_out):
    dma = pltpu.SemaphoreType.DMA
    hbm = pl.BlockSpec(memory_space=pl.ANY)
    vmem = pl.BlockSpec(memory_space=pltpu.VMEM)
    return pl.pallas_call(
        kernel,
        out_shape=jax.ShapeDtypeStruct((ROWS, WIDTH), BF16),
        in_specs=[hbm, hbm, hbm, vmem, vmem, vmem, hbm],
        out_specs=vmem,
        scratch_shapes=[
            pltpu.VMEM((3, ROWS, WIDTH), BF16),
            pltpu.VMEM((TILES, ROWS, LANES), F32),
            pltpu.VMEM((TILES, ROWS, LANES), F32),
            pltpu.VMEM((TILES, MODES * SUB, LANES), F32),
            pltpu.VMEM((TILES, MODES * SUB, LANES), F32),
            pltpu.VMEM((TILES, SUB, LANES), F32),
            pltpu.VMEM((TILES, MODES * SUB, LANES), F32),
            pltpu.VMEM((TILES, MODES * SUB, LANES), F32),
            pltpu.VMEM((8, MODES, WIDTH), F32),
            pltpu.VMEM((ROWS, 4 * WIDTH), BF16),
            pltpu.VMEM((4, 4 * WIDTH, WIDTH), BF16),
            pltpu.VMEM((ROWS, WIDTH), BF16),
            pltpu.VMEM((ROWS, WIDTH), BF16),
            pltpu.VMEM((2, ROWS, WIDTH), BF16),
            pltpu.VMEM((2, ROWS, WIDTH), BF16),
            pltpu.VMEM((TILES, CHUNK, LANES), F32),
            dma((3,)), dma((4,)), dma((4,)), dma((4,)),
            dma((4, 2)), dma((4, 2)), dma((4, 2)), dma((4, 2)),
            dma((8,)), dma((8,)),
            dma((CHUNKS,)), dma((CHUNKS,)), dma((CHUNKS,)), dma((CHUNKS,)),
            dma((CHUNKS,)), dma((CHUNKS,)),
            dma((2, CHUNKS)), dma((2, CHUNKS)), dma((2, CHUNKS)), dma((2, CHUNKS)),
        ],
        compiler_params=pltpu.CompilerParams(
            collective_id=0, has_side_effects=True, vmem_limit_bytes=48 << 20
        ),
        cost_estimate=pl.CostEstimate(
            flops=2 * ROWS * 16 * WIDTH * WIDTH, bytes_accessed=13 << 20, transcendentals=0
        ),
        name="layer",
    )(query_rows, key_rows, value_rows, horizon, residue, skip.reshape(1, WIDTH), w_out)


def solution(mesh):
    in_specs = (
        P("seq", "chan"),
        P("seq", "chan"),
        P("seq", "chan"),
        P(None, "chan"),
        P(None, "chan"),
        P("chan"),
        P("chan", None),
    )
    out_specs = P("seq", "chan")
    return jax.shard_map(local, mesh=mesh, in_specs=in_specs, out_specs=out_specs, check_vma=False)
```

time: 512 us -> 100 us (0.20)
  waiting for transfers between devices: 195 us -> 0 us
  local copies, waits for them, and re-layouts: 123 us -> 6.84 us
  Pallas kernels: 0 us -> 93.1 us
  matrix products: 89.9 us -> 0 us
  blocking collectives: 63.1 us -> 0 us
  other arithmetic: 24.9 us -> 0 us
  between operations: 13.5 us -> 0.02 us
    reduce_scatter x1 -> x0, waiting for transfers between devices: 195 us -> none  [local(): lax.psum_scatter(lax.dot_general(w_out, gated, (((0,), (1,)), ((), ())),...]
    gather x2 -> x0, local copies, waits for them, and re-layouts: 99.9 us -> none  [local(): jnp.take(kernel, jnp.maximum(lags, 0), axis=0)]
    pallas_call x0 -> x1, Pallas kernels: none -> 93.1 us  [local(): pl.pallas_call(kernel, out_shape=jax.ShapeDtypeStruct((ROWS, WIDTH), BF16...]
    dot_general x4 -> x0, matrix products: 89.9 us -> none  [the longest x1 55.9 us: local(): jnp.einsum('tsc,nsc->ntc', toeplitz, pieces, precision=lax.Precision.HIGH...]
    all_gather x2 -> x0, blocking collectives: 63.1 us -> none  [entering(): pieces = jax.tree.map(lambda part: lax.all_gather(part, axis), value)]
    exp x1 -> x0, other arithmetic: 7.63 us -> none  [local(): powers = jnp.exp(-rate[:, None, :] * offsets[None, :, None])]
    rev x1 -> x0, local copies, waits for them, and re-layouts: 7.34 us -> none  [local(): powers[:, ::-1, :]]
    select_n x7 -> x0, other arithmetic: 5.52 us -> none  [hop(): jnp.where(position < mine, new, old)]
  transfers between devices with their start and end apart: 1 -> 0, of which waited for: 1 -> 0; matrix products, arithmetic and copies ran while one was open for 0% -> 0% of each run, Pallas kernels for 0% -> 0%
where the time goes in v1:
time: 100 us
  Pallas kernels  93.1 us (93%)
  local copies, waits for them, and re-layouts  6.84 us (7%)
    pallas_call x1, Pallas kernels, local(): pl.pallas_call(kernel, out_shape=jax.ShapeDtypeStruct((ROWS, WIDTH), BF16...  93.1 us
    unnamed x13, local copies, waits for them, and re-layouts  6.84 us

profile of v1, /device:TPU:1, one launch (start us, length us, event | category | flops | bytes accessed | tf_op | source)
XLA Modules:
  0.0 100.0 jit_solution(16753185330678058203)
XLA Ops:
  0.0 0.0 copy-start
  0.0 1.2 %copy-done = bf16[1024,512]{1,0:T(8,128)(2,1)S(1)} copy-done((bf16[1024,512]{1,0:T(8,128)(2,1)S(1)}, bf16[1024,512]{1,0:T(8,128)(2,1)}, u32[]{:S(2)}) %copy-start) | copy-done | bytes 1048600
  1.2 0.0 copy-start.1
  1.2 1.2 %copy-done.1 = bf16[1024,512]{1,0:T(8,128)(2,1)S(1)} copy-done((bf16[1024,512]{1,0:T(8,128)(2,1)S(1)}, bf16[1024,512]{1,0:T(8,128)(2,1)}, u32[]{:S(2)}) %copy-start.1) | copy-done | bytes 1048600
  2.5 0.0 copy-start.2
  2.5 1.2 %copy-done.2 = bf16[1024,512]{1,0:T(8,128)(2,1)S(1)} copy-done((bf16[1024,512]{1,0:T(8,128)(2,1)S(1)}, bf16[1024,512]{1,0:T(8,128)(2,1)}, u32[]{:S(2)}) %copy-start.2) | copy-done | bytes 1048600
  3.7 0.0 copy-start.3
  3.7 0.8 copy-done.3
  4.4 0.0 copy-start.4
  4.4 0.8 copy-done.4
  5.2 0.0 copy-start.5
  5.2 0.7 copy-done.5
  5.9 93.1 %layer.1 = bf16[1024,512]{1,0:T(8,128)(2,1)S(1)} custom-call(bf16[1024,512]{1,0:T(8,128)(2,1)S(1)} %copy-done, bf16[1024,512]{1,0:T(8,128)(2,1)S(1)} %copy-done.1, bf16[1024,512]{1,0:T(8,128)(2,1)S(1)} %copy-done.2, f32[16,512]{1,0:T(8,128)S(1)} %copy-done.3, f32[16,512]{1,0:T(8,128)S(1)} %copy-done.4, f32[1,512]{1,0:T(1,128)S(1)} %bitcast.1, ...), custom_call_target="tpu_custom_call" | custom-call | flops 8589934592 | bytes 13631488 | tf_op jit(solution)/shard_map/layer/pallas_call | solution.py:392
  99.0 1.0 copy.9
Async XLA Ops:
  0.0 1.2 %copy-start = (bf16[1024,512]{1,0:T(8,128)(2,1)S(1)}, bf16[1024,512]{1,0:T(8,128)(2,1)}, u32[]{:S(2)}) copy-start(bf16[1024,512]{1,0:T(8,128)(2,1)} %q_hbm.1) | copy-start | bytes 3145732
  1.2 1.2 %copy-start.1 = (bf16[1024,512]{1,0:T(8,128)(2,1)S(1)}, bf16[1024,512]{1,0:T(8,128)(2,1)}, u32[]{:S(2)}) copy-start(bf16[1024,512]{1,0:T(8,128)(2,1)} %k_hbm.1) | copy-start | bytes 3145732
  2.5 1.2 %copy-start.2 = (bf16[1024,512]{1,0:T(8,128)(2,1)S(1)}, bf16[1024,512]{1,0:T(8,128)(2,1)}, u32[]{:S(2)}) copy-start(bf16[1024,512]{1,0:T(8,128)(2,1)} %v_hbm.1) | copy-start | bytes 3145732
  3.7 0.8 copy-start.3
  4.4 0.8 copy-start.4
  5.2 0.7 copy-start.5

commit v2 on v1

--- a/solution.py
+++ b/solution.py
@@ -20,9 +20,10 @@
 TILES = WIDTH // LANES
 CHUNKS = 8
 CHUNK = ROWS // CHUNKS
-LAG2 = 2
-LAG3 = 4
-VIA = {2: (0, 1), 1: (0, 1), 3: (0, 1), 0: (1, 1)}
+LAG_UP = 2
+LAG_DOWN = 5
+LAG_LAST = 7
+VIA = {2: (0, 1), 1: (0, 1), 3: (1, 1), 0: (0, 1)}
 ORDER = (2, 1, 3, 0)
 
 
@@ -31,10 +32,10 @@
 
 
 def kernel(
-    q_hbm, k_hbm, v_hbm, horizon_ref, residue_ref, skip_ref, w_hbm, out_ref,
-    stage, mix, gate, decay, coef, skips, local, begin, ends, gat, wn,
+    q_hbm, k_hbm, v_hbm, horizon_hbm, residue_hbm, skip_hbm, w_hbm, out_ref,
+    stage, horizon_ref, residue_ref, skip_ref, mix, gate, decay, coef, skips, local, begin, ends, gat, wn,
     first_out, first_in, second_out, second_in, total,
-    stage_sem, wl, wc_s, wc_r, wx_s, wx_r, wy_s, wy_r, st_s, st_r,
+    stage_sem, small_sem, wl, wc_s, wc_r, wx_s, wx_r, wy_s, wy_r, st_s, st_r,
     gc_s, gc_r, gx_s, gx_r, gf_s, gf_r, f_s, f_r, s_s, s_r,
 ):
     seq = lax.axis_index("seq")
@@ -67,7 +68,13 @@
         pltpu.make_async_copy(src, stage.at[i], stage_sem.at[i])
         for i, src in enumerate((k_hbm, v_hbm, q_hbm))
     ]
-    for load in loads:
+    small = [
+        pltpu.make_async_copy(src, dst, small_sem.at[i])
+        for i, (src, dst) in enumerate(
+            ((horizon_hbm, horizon_ref), (residue_hbm, residue_ref), (skip_hbm, skip_ref))
+        )
+    ]
+    for load in small + loads:
         load.start()
 
     def remote(src, dst, send, recv, device):
@@ -110,14 +117,15 @@
         )
 
     pl.semaphore_wait(barrier, len(peers))
-    for d in ORDER:
-        for c in (0, 1):
-            w_x(d, c).start()
+    for c in (0, 1):
+        w_x(2, c).start()
     for d in ORDER:
         w_mate(d).start()
     for d in ORDER:
         w_own(d).start()
 
+    for load in small:
+        load.wait()
     rate = 1.0 / horizon_ref[...]
     twice = 2.0 * rate
     series = jnp.ones_like(twice)
@@ -180,6 +188,8 @@
 
     for k in range(1, 8):
         state_copy(k).start()
+    for d, c in ((1, 0), (1, 1), (3, 0), (3, 1), (0, 1)):
+        w_x(d, c).start()
 
     loads[2].wait()
     for t in range(TILES):
@@ -196,6 +206,7 @@
 
     for k in range(1, 8):
         state_copy(k).wait_recv()
+    pass_on(2)
     incoming = jnp.zeros((MODES, WIDTH), F32)
     for k in range(7, 0, -1):
         incoming = jnp.where(k <= seq, device_decay * incoming + ends[k], incoming)
@@ -267,7 +278,7 @@
         return carry
 
     lax.fori_loop(0, CHUNKS, filter_chunk, 0)
-    pass_on(2)
+    w_x(0, 0).start()
     pass_on(1)
 
     def w_ready(d):
@@ -301,16 +312,15 @@
         for side in (0, 1):
             first_copy(r, side).start()
 
-    def second_sum(r):
-        for side in (0, 1):
-            part = pl.ds(side * half, half)
-            rest = pl.ds((1 - side) * half, half)
-            partial = product(r, 3 if side else 1)
-            first_copy(r, side).wait_recv()
-            summed = partial[:, side * half:(side + 1) * half] + first_in[chunk_rows(r), part].astype(F32)
-            second_out[side, chunk_rows(r), part] = summed.astype(BF16)
-            second_out[side, chunk_rows(r), rest] = partial[:, (1 - side) * half:(2 - side) * half].astype(BF16)
-            second_copy(r, side).start()
+    def second_sum(r, side):
+        part = pl.ds(side * half, half)
+        rest = pl.ds((1 - side) * half, half)
+        partial = product(r, 3 if side else 1)
+        first_copy(r, side).wait_recv()
+        summed = partial[:, side * half:(side + 1) * half] + first_in[chunk_rows(r), part].astype(F32)
+        second_out[side, chunk_rows(r), part] = summed.astype(BF16)
+        second_out[side, chunk_rows(r), rest] = partial[:, (1 - side) * half:(2 - side) * half].astype(BF16)
+        second_copy(r, side).start()
 
     def last_sum(r):
         own = product(r, 0)
@@ -336,34 +346,41 @@
         def _():
             first_sum(i)
 
-        @pl.when(i == LAG2 - 1)
+        @pl.when(i == LAG_UP)
+        def _():
+            w_ready(1)
+
+        @pl.when((i >= LAG_UP) & (i < CHUNKS + LAG_UP))
+        def _():
+            second_sum(i - LAG_UP, 0)
+
+        @pl.when(i == LAG_DOWN - 2)
         def _():
             pass_on(3)
 
-        @pl.when(i == LAG2)
-        def _():
-            w_ready(1)
+        @pl.when(i == LAG_DOWN)
+        def _():
             w_ready(3)
 
-        @pl.when((i >= LAG2) & (i < CHUNKS + LAG2))
-        def _():
-            second_sum(i - LAG2)
-
-        @pl.when(i == LAG3 - 1)
+        @pl.when((i >= LAG_DOWN) & (i < CHUNKS + LAG_DOWN))
+        def _():
+            second_sum(i - LAG_DOWN, 1)
+
+        @pl.when(i == LAG_LAST - 1)
         def _():
             pass_on(0)
 
-        @pl.when(i == LAG3)
+        @pl.when(i == LAG_LAST)
         def _():
             w_ready(0)
 
-        @pl.when(i >= LAG3)
-        def _():
-            last_sum(i - LAG3)
+        @pl.when(i >= LAG_LAST)
+        def _():
+            last_sum(i - LAG_LAST)
 
         return carry
 
-    lax.fori_loop(0, CHUNKS + LAG3, turn, 0)
+    lax.fori_loop(0, CHUNKS + LAG_LAST, turn, 0)
 
     for d in ORDER:
         for c in (0, 1):
@@ -387,15 +404,18 @@
 
 def local(query_rows, key_rows, value_rows, horizon, residue, skip, w_out):
     dma = pltpu.SemaphoreType.DMA
-    hbm = pl.BlockSpec(memory_space=pl.ANY)
+    hbm = pl.BlockSpec(memory_space=pltpu.HBM)
     vmem = pl.BlockSpec(memory_space=pltpu.VMEM)
     return pl.pallas_call(
         kernel,
         out_shape=jax.ShapeDtypeStruct((ROWS, WIDTH), BF16),
-        in_specs=[hbm, hbm, hbm, vmem, vmem, vmem, hbm],
+        in_specs=[hbm] * 7,
         out_specs=vmem,
         scratch_shapes=[
             pltpu.VMEM((3, ROWS, WIDTH), BF16),
+            pltpu.VMEM((MODES, WIDTH), F32),
+            pltpu.VMEM((MODES, WIDTH), F32),
+            pltpu.VMEM((1, WIDTH), F32),
             pltpu.VMEM((TILES, ROWS, LANES), F32),
             pltpu.VMEM((TILES, ROWS, LANES), F32),
             pltpu.VMEM((TILES, MODES * SUB, LANES), F32),
@@ -411,7 +431,7 @@
             pltpu.VMEM((2, ROWS, WIDTH), BF16),
             pltpu.VMEM((2, ROWS, WIDTH), BF16),
             pltpu.VMEM((TILES, CHUNK, LANES), F32),
-            dma((3,)), dma((4,)), dma((4,)), dma((4,)),
+            dma((3,)), dma((3,)), dma((4,)), dma((4,)), dma((4,)),
             dma((4, 2)), dma((4, 2)), dma((4, 2)), dma((4, 2)),
             dma((8,)), dma((8,)),
             dma((CHUNKS,)), dma((CHUNKS,)), dma((CHUNKS,)), dma((CHUNKS,)),

time: 100 us -> 82.1 us (0.82); the launches traced: 100 us -> 80.7 us
  Pallas kernels: 93.1 us -> 73.8 us
    pallas_call x1, Pallas kernels: 93.1 us -> 73.8 us  [local(): pl.pallas_call(kernel, out_shape=jax.ShapeDtypeStruct((ROWS, WIDTH), BF16...]
where the time goes in v2:
time: 82.1 us; the launch traced here: 80.7 us
  Pallas kernels  73.8 us (90%)
  local copies, waits for them, and re-layouts  6.84 us (8%)
    pallas_call x1, Pallas kernels, local(): pl.pallas_call(kernel, out_shape=jax.ShapeDtypeStruct((ROWS, WIDTH), BF16...  73.8 us
    unnamed x13, local copies, waits for them, and re-layouts  6.84 us

profile of v2, /device:TPU:1, one launch (start us, length us, event | category | flops | bytes accessed | tf_op | source)
XLA Modules:
  0.0 80.7 jit_solution(14497631355794906999)
XLA Ops:
  0.0 0.0 copy-start
  0.0 1.2 %copy-done = bf16[1024,512]{1,0:T(8,128)(2,1)S(1)} copy-done((bf16[1024,512]{1,0:T(8,128)(2,1)S(1)}, bf16[1024,512]{1,0:T(8,128)(2,1)}, u32[]{:S(2)}) %copy-start) | copy-done | bytes 1048600
  1.2 0.0 copy-start.1
  1.2 1.2 %copy-done.1 = bf16[1024,512]{1,0:T(8,128)(2,1)S(1)} copy-done((bf16[1024,512]{1,0:T(8,128)(2,1)S(1)}, bf16[1024,512]{1,0:T(8,128)(2,1)}, u32[]{:S(2)}) %copy-start.1) | copy-done | bytes 1048600
  2.5 0.0 copy-start.2
  2.5 1.2 %copy-done.2 = bf16[1024,512]{1,0:T(8,128)(2,1)S(1)} copy-done((bf16[1024,512]{1,0:T(8,128)(2,1)S(1)}, bf16[1024,512]{1,0:T(8,128)(2,1)}, u32[]{:S(2)}) %copy-start.2) | copy-done | bytes 1048600
  3.7 0.0 copy-start.3
  3.7 0.8 copy-done.3
  4.4 0.0 copy-start.4
  4.4 0.8 copy-done.4
  5.2 0.0 copy-start.5
  5.2 0.7 copy-done.5
  5.9 73.8 %layer.1 = bf16[1024,512]{1,0:T(8,128)(2,1)S(1)} custom-call(bf16[1024,512]{1,0:T(8,128)(2,1)S(1)} %copy-done, bf16[1024,512]{1,0:T(8,128)(2,1)S(1)} %copy-done.1, bf16[1024,512]{1,0:T(8,128)(2,1)S(1)} %copy-done.2, f32[16,512]{1,0:T(8,128)S(1)} %copy-done.3, f32[16,512]{1,0:T(8,128)S(1)} %copy-done.4, f32[1,512]{1,0:T(1,128)S(1)} %bitcast.1, ...), custom_call_target="tpu_custom_call" | custom-call | flops 8589934592 | bytes 13631488 | tf_op jit(solution)/shard_map/layer/pallas_call | solution.py:409
  79.7 1.0 %copy.9 = bf16[1024,512]{1,0:T(8,128)(2,1)} copy(bf16[1024,512]{1,0:T(8,128)(2,1)S(1)} %layer.1) | data formatting | bytes 2097152
Async XLA Ops:
  0.0 1.2 %copy-start = (bf16[1024,512]{1,0:T(8,128)(2,1)S(1)}, bf16[1024,512]{1,0:T(8,128)(2,1)}, u32[]{:S(2)}) copy-start(bf16[1024,512]{1,0:T(8,128)(2,1)} %q_hbm.1) | copy-start | bytes 3145732
  1.2 1.2 %copy-start.1 = (bf16[1024,512]{1,0:T(8,128)(2,1)S(1)}, bf16[1024,512]{1,0:T(8,128)(2,1)}, u32[]{:S(2)}) copy-start(bf16[1024,512]{1,0:T(8,128)(2,1)} %k_hbm.1) | copy-start | bytes 3145732
  2.5 1.2 %copy-start.2 = (bf16[1024,512]{1,0:T(8,128)(2,1)S(1)}, bf16[1024,512]{1,0:T(8,128)(2,1)}, u32[]{:S(2)}) copy-start(bf16[1024,512]{1,0:T(8,128)(2,1)} %v_hbm.1) | copy-start | bytes 3145732
  3.7 0.8 copy-start.3
  4.4 0.8 copy-start.4
  5.2 0.7 copy-start.5

commit v3 on v2

--- a/solution.py
+++ b/solution.py
@@ -20,10 +20,10 @@
 TILES = WIDTH // LANES
 CHUNKS = 8
 CHUNK = ROWS // CHUNKS
-LAG_UP = 2
-LAG_DOWN = 5
-LAG_LAST = 7
-VIA = {2: (0, 1), 1: (0, 1), 3: (1, 1), 0: (0, 1)}
+EARLY = 6
+UP = 2
+DOWN = 6
+VIA = {2: (0, 1), 1: (0, 1), 3: (1, 1), 0: (1, 1)}
 ORDER = (2, 1, 3, 0)
 
 
@@ -188,7 +188,7 @@
 
     for k in range(1, 8):
         state_copy(k).start()
-    for d, c in ((1, 0), (1, 1), (3, 0), (3, 1), (0, 1)):
+    for d, c in ((1, 0), (1, 1), (3, 0), (3, 1), (0, 0), (0, 1)):
         w_x(d, c).start()
 
     loads[2].wait()
@@ -199,14 +199,14 @@
                 stage[2, pl.ds(n * BLOCK, BLOCK), lane].astype(F32)
             )
 
-    def pass_on(d):
-        for c in (0, 1):
-            w_x(d, c).wait_recv()
-            w_y(d, c).start()
+    def pass_on(d, c):
+        w_x(d, c).wait_recv()
+        w_y(d, c).start()
 
     for k in range(1, 8):
         state_copy(k).wait_recv()
-    pass_on(2)
+    pass_on(2, 0)
+    pass_on(2, 1)
     incoming = jnp.zeros((MODES, WIDTH), F32)
     for k in range(7, 0, -1):
         incoming = jnp.where(k <= seq, device_decay * incoming + ends[k], incoming)
@@ -278,8 +278,8 @@
         return carry
 
     lax.fori_loop(0, CHUNKS, filter_chunk, 0)
-    w_x(0, 0).start()
-    pass_on(1)
+    pass_on(1, 0)
+    pass_on(1, 1)
 
     def w_ready(d):
         for c in (0, 1):
@@ -290,11 +290,9 @@
     def product(r, d):
         return jnp.dot(gat[chunk_rows(r), :], wn[d], preferred_element_type=F32)
 
-    def first_copy(r, side):
-        part = pl.ds(side * half, half)
-        return remote(
-            first_out.at[chunk_rows(r), part], first_in.at[chunk_rows(r), part],
-            f_s.at[side, r], f_r.at[side, r], z_down if side else z_up,
+    def first_copy(r, device):
+        return remote(
+            first_out.at[chunk_rows(r)], first_in.at[chunk_rows(r)], f_s.at[r], f_r.at[r], device
         )
 
     def second_copy(r, side):
@@ -309,17 +307,30 @@
         g_mate(r).wait_recv()
         g_pass(r).wait_recv()
         first_out[chunk_rows(r), :] = product(r, 2).astype(BF16)
-        for side in (0, 1):
-            first_copy(r, side).start()
+
+        @pl.when(r < EARLY)
+        def _():
+            first_copy(r, z_down).start()
+
+        @pl.when(r >= EARLY)
+        def _():
+            first_copy(r, z_up).start()
 
     def second_sum(r, side):
-        part = pl.ds(side * half, half)
-        rest = pl.ds((1 - side) * half, half)
         partial = product(r, 3 if side else 1)
-        first_copy(r, side).wait_recv()
-        summed = partial[:, side * half:(side + 1) * half] + first_in[chunk_rows(r), part].astype(F32)
-        second_out[side, chunk_rows(r), part] = summed.astype(BF16)
-        second_out[side, chunk_rows(r), rest] = partial[:, (1 - side) * half:(2 - side) * half].astype(BF16)
+        passes = r < EARLY if side else r >= EARLY
+
+        @pl.when(passes)
+        def _():
+            first_copy(r, z_up).wait_recv()
+            second_out[side, chunk_rows(r), :] = (
+                partial + first_in[chunk_rows(r), :].astype(F32)
+            ).astype(BF16)
+
+        @pl.when(jnp.logical_not(passes))
+        def _():
+            second_out[side, chunk_rows(r), :] = partial.astype(BF16)
+
         second_copy(r, side).start()
 
     def last_sum(r):
@@ -337,50 +348,42 @@
                     total[t, pl.ds(n, piece, stride=SUB), :].astype(BF16)
                 )
 
+    def between(first, last, body):
+        def step(r, carry):
+            body(r)
+            return carry
+
+        lax.fori_loop(first, last, step, 0)
+
     def turn(i, carry):
+        for at, d, c in ((2, 3, 0), (4, 3, 1), (6, 0, 0)):
+            @pl.when(i == at)
+            def _(d=d, c=c):
+                pass_on(d, c)
+
         @pl.when(i == 0)
         def _():
             w_ready(2)
 
-        @pl.when(i < CHUNKS)
-        def _():
-            first_sum(i)
-
-        @pl.when(i == LAG_UP)
-        def _():
-            w_ready(1)
-
-        @pl.when((i >= LAG_UP) & (i < CHUNKS + LAG_UP))
-        def _():
-            second_sum(i - LAG_UP, 0)
-
-        @pl.when(i == LAG_DOWN - 2)
-        def _():
-            pass_on(3)
-
-        @pl.when(i == LAG_DOWN)
-        def _():
-            w_ready(3)
-
-        @pl.when((i >= LAG_DOWN) & (i < CHUNKS + LAG_DOWN))
-        def _():
-            second_sum(i - LAG_DOWN, 1)
-
-        @pl.when(i == LAG_LAST - 1)
-        def _():
-            pass_on(0)
-
-        @pl.when(i == LAG_LAST)
-        def _():
-            w_ready(0)
-
-        @pl.when(i >= LAG_LAST)
-        def _():
-            last_sum(i - LAG_LAST)
-
+        first_sum(i)
+
+        for at, d in ((UP, 1), (DOWN, 3)):
+            @pl.when(i == at)
+            def _(d=d):
+                w_ready(d)
+
+        upward = (i >= UP) & (i < EARLY)
+        between(jnp.where(i == UP, 0, i), jnp.where(upward, i + 1, 0), lambda r: second_sum(r, 0))
+        downward = 2 * jnp.maximum(i - DOWN, 0)
+        between(downward, jnp.where(i < DOWN, 0, downward + 2), lambda r: second_sum(r, 1))
         return carry
 
-    lax.fori_loop(0, CHUNKS + LAG_LAST, turn, 0)
+    lax.fori_loop(0, CHUNKS, turn, 0)
+    pass_on(0, 1)
+    between(2 * (CHUNKS - DOWN), CHUNKS, lambda r: second_sum(r, 1))
+    between(EARLY, CHUNKS, lambda r: second_sum(r, 0))
+    w_ready(0)
+    between(0, CHUNKS, last_sum)
 
     for d in ORDER:
         for c in (0, 1):
@@ -394,8 +397,8 @@
         g_x(r).wait_send()
         g_mate(r).wait_send()
         g_pass(r).wait_send()
+        first_copy(r, z_up).wait_send()
         for side in (0, 1):
-            first_copy(r, side).wait_send()
             second_copy(r, side).wait_send()
         return carry
 
@@ -436,10 +439,10 @@
             dma((8,)), dma((8,)),
             dma((CHUNKS,)), dma((CHUNKS,)), dma((CHUNKS,)), dma((CHUNKS,)),
             dma((CHUNKS,)), dma((CHUNKS,)),
-            dma((2, CHUNKS)), dma((2, CHUNKS)), dma((2, CHUNKS)), dma((2, CHUNKS)),
+            dma((CHUNKS,)), dma((CHUNKS,)), dma((2, CHUNKS)), dma((2, CHUNKS)),
         ],
         compiler_params=pltpu.CompilerParams(
-            collective_id=0, has_side_effects=True, vmem_limit_bytes=48 << 20
+            collective_id=0, has_side_effects=True, vmem_limit_bytes=60 << 20
         ),
         cost_estimate=pl.CostEstimate(
             flops=2 * ROWS * 16 * WIDTH * WIDTH, bytes_accessed=13 << 20, transcendentals=0

time: 82.1 us -> 75.8 us (0.923); the launches traced: 80.7 us -> 75.7 us
  local copies, waits for them, and re-layouts: 6.84 us -> 2.26 us
    unnamed x13 -> x1, local copies, waits for them, and re-layouts: 6.84 us -> 2.26 us
where the time goes in v3:
time: 75.8 us; the launch traced here: 75.7 us
  Pallas kernels  73.4 us (97%)
  local copies, waits for them, and re-layouts  2.26 us (3%)
    pallas_call x1, Pallas kernels, local(): pl.pallas_call(kernel, out_shape=jax.ShapeDtypeStruct((ROWS, WIDTH), BF16...  73.4 us
    unnamed x1, local copies, waits for them, and re-layouts  2.26 us

profile of v3, /device:TPU:1, one launch (start us, length us, event | category | flops | bytes accessed | tf_op | source)
XLA Modules:
  0.0 75.7 jit_solution(12140505074980648382)
XLA Ops:
  0.0 73.4 %layer.1 = bf16[1024,512]{1,0:T(8,128)(2,1)} custom-call(bf16[1024,512]{1,0:T(8,128)(2,1)} %q_hbm.1, bf16[1024,512]{1,0:T(8,128)(2,1)} %k_hbm.1, bf16[1024,512]{1,0:T(8,128)(2,1)} %v_hbm.1, f32[16,512]{1,0:T(8,128)} %horizon_hbm.1, f32[16,512]{1,0:T(8,128)} %residue_hbm.1, f32[1,512]{1,0:T(1,128)} %bitcast.1, bf16[512,8192]{1,0:T(8,128)(2,1)} %w_hbm.1), custom_call_target="tpu_custom_call" | custom-call | flops 8589934592 | bytes 13631488 | tf_op jit(solution)/shard_map/layer/pallas_call | solution.py:412
  73.4 2.3 %copy.9 = bf16[1024,512]{1,0:T(8,128)(2,1)} copy(bf16[1024,512]{1,0:T(8,128)(2,1)} %layer.1) | data formatting | bytes 2097152

commit v4 on v3

--- a/solution.py
+++ b/solution.py
@@ -20,7 +20,7 @@
 TILES = WIDTH // LANES
 CHUNKS = 8
 CHUNK = ROWS // CHUNKS
-EARLY = 6
+EARLY = 5
 UP = 2
 DOWN = 6
 VIA = {2: (0, 1), 1: (0, 1), 3: (1, 1), 0: (1, 1)}
@@ -34,7 +34,7 @@
 def kernel(
     q_hbm, k_hbm, v_hbm, horizon_hbm, residue_hbm, skip_hbm, w_hbm, out_ref,
     stage, horizon_ref, residue_ref, skip_ref, mix, gate, decay, coef, skips, local, begin, ends, gat, wn,
-    first_out, first_in, second_out, second_in, total,
+    first_out, first_in, second_out, second_in, near, total,
     stage_sem, small_sem, wl, wc_s, wc_r, wx_s, wx_r, wy_s, wy_r, st_s, st_r,
     gc_s, gc_r, gx_s, gx_r, gf_s, gf_r, f_s, f_r, s_s, s_r,
 ):
@@ -88,21 +88,21 @@
         return pl.ds(pl.multiple_of(block * WIDTH, WIDTH), WIDTH)
 
     half = WIDTH // 2
-
-    def half_rows(c, p):
-        return pl.ds(pl.multiple_of((2 + c) * WIDTH + p * half, half), half)
-
-    def w_x(d, c):
-        return remote(
-            w_hbm.at[pl.ds(pl.multiple_of(parity * half, half), half),
-                     columns(1 - xl, d, lax.rem(core + c, 2))],
-            wn.at[d, half_rows(c, parity)],
-            wx_s.at[d, c], wx_r.at[d, c], x_side(VIA[d][c], c),
-        )
-
-    def w_y(d, c):
-        piece = wn.at[d, half_rows(c, parity)]
-        return remote(piece, piece, wy_s.at[d, c], wy_r.at[d, c], y_up if c else y_down)
+    part = half // 2
+
+    def part_rows(first, h):
+        return pl.ds(pl.multiple_of(first + parity * half + h * part, part), part)
+
+    def w_x(d, c, h):
+        return remote(
+            w_hbm.at[part_rows(0, h), columns(1 - xl, d, lax.rem(core + c, 2))],
+            wn.at[d, part_rows((2 + c) * WIDTH, h)],
+            wx_s.at[d, c, h], wx_r.at[d, c, h], x_side(VIA[d][c], c),
+        )
+
+    def w_y(d, c, h):
+        piece = wn.at[d, part_rows((2 + c) * WIDTH, h)]
+        return remote(piece, piece, wy_s.at[d, c, h], wy_r.at[d, c, h], y_up if c else y_down)
 
     def w_mate(d):
         return remote(
@@ -118,7 +118,8 @@
 
     pl.semaphore_wait(barrier, len(peers))
     for c in (0, 1):
-        w_x(2, c).start()
+        for h in (0, 1):
+            w_x(2, c, h).start()
     for d in ORDER:
         w_mate(d).start()
     for d in ORDER:
@@ -189,7 +190,8 @@
     for k in range(1, 8):
         state_copy(k).start()
     for d, c in ((1, 0), (1, 1), (3, 0), (3, 1), (0, 0), (0, 1)):
-        w_x(d, c).start()
+        for h in (0, 1):
+            w_x(d, c, h).start()
 
     loads[2].wait()
     for t in range(TILES):
@@ -199,9 +201,10 @@
                 stage[2, pl.ds(n * BLOCK, BLOCK), lane].astype(F32)
             )
 
-    def pass_on(d, c):
-        w_x(d, c).wait_recv()
-        w_y(d, c).start()
+    def pass_on(d, c, parts=(0, 1)):
+        for h in parts:
+            w_x(d, c, h).wait_recv()
+            w_y(d, c, h).start()
 
     for k in range(1, 8):
         state_copy(k).wait_recv()
@@ -283,13 +286,18 @@
 
     def w_ready(d):
         for c in (0, 1):
-            w_y(d, c).wait_recv()
-        w_mate(d).wait_recv()
-        w_own(d).wait()
+            for h in (0, 1):
+                w_y(d, c, h).wait_recv()
 
     def product(r, d):
         return jnp.dot(gat[chunk_rows(r), :], wn[d], preferred_element_type=F32)
 
+    def near_product(b):
+        rows = pl.ds(pl.multiple_of(b * 256, 256), 256)
+        near[rows, :] = jnp.dot(
+            gat[rows, 0:2 * WIDTH], wn[0, 0:2 * WIDTH, :], preferred_element_type=F32
+        )
+
     def first_copy(r, device):
         return remote(
             first_out.at[chunk_rows(r)], first_in.at[chunk_rows(r)], f_s.at[r], f_r.at[r], device
@@ -302,8 +310,6 @@
         )
 
     def first_sum(r):
-        g_x(r).wait_recv()
-        g_pass(r).start()
         g_mate(r).wait_recv()
         g_pass(r).wait_recv()
         first_out[chunk_rows(r), :] = product(r, 2).astype(BF16)
@@ -334,7 +340,10 @@
         second_copy(r, side).start()
 
     def last_sum(r):
-        own = product(r, 0)
+        own = near[chunk_rows(r), :] + jnp.dot(
+            gat[chunk_rows(r), 2 * WIDTH:4 * WIDTH], wn[0, 2 * WIDTH:4 * WIDTH, :],
+            preferred_element_type=F32,
+        )
         for side in (0, 1):
             second_copy(r, side).wait_recv()
         own = own + second_in[0, chunk_rows(r), :].astype(F32) + second_in[1, chunk_rows(r), :].astype(F32)
@@ -356,39 +365,43 @@
         lax.fori_loop(first, last, step, 0)
 
     def turn(i, carry):
-        for at, d, c in ((2, 3, 0), (4, 3, 1), (6, 0, 0)):
+        for at, c, parts in ((2, 0, (0, 1)), (3, 1, (0,)), (4, 1, (1,))):
             @pl.when(i == at)
-            def _(d=d, c=c):
-                pass_on(d, c)
-
-        @pl.when(i == 0)
-        def _():
-            w_ready(2)
-
-        first_sum(i)
-
-        for at, d in ((UP, 1), (DOWN, 3)):
+            def _(c=c, parts=parts):
+                pass_on(3, c, parts)
+
+        g_x(i).wait_recv()
+        g_pass(i).start()
+
+        for at, d in ((0, 2), (UP, 1), (DOWN, 3)):
             @pl.when(i == at)
             def _(d=d):
                 w_ready(d)
 
-        upward = (i >= UP) & (i < EARLY)
-        between(jnp.where(i == UP, 0, i), jnp.where(upward, i + 1, 0), lambda r: second_sum(r, 0))
+        upward = (i >= UP) & (i <= EARLY)
+        between(jnp.where(i == UP, 0, jnp.maximum(i - 1, 0)), jnp.where(upward, i, 0), lambda r: second_sum(r, 0))
         downward = 2 * jnp.maximum(i - DOWN, 0)
         between(downward, jnp.where(i < DOWN, 0, downward + 2), lambda r: second_sum(r, 1))
+        first_sum(i)
         return carry
 
+    for d in ORDER:
+        w_mate(d).wait_recv()
+        w_own(d).wait()
     lax.fori_loop(0, CHUNKS, turn, 0)
+    pass_on(0, 0)
+    between(2 * (CHUNKS - DOWN), CHUNKS, lambda r: second_sum(r, 1))
     pass_on(0, 1)
-    between(2 * (CHUNKS - DOWN), CHUNKS, lambda r: second_sum(r, 1))
+    between(0, ROWS // 256, near_product)
     between(EARLY, CHUNKS, lambda r: second_sum(r, 0))
     w_ready(0)
     between(0, CHUNKS, last_sum)
 
     for d in ORDER:
         for c in (0, 1):
-            w_x(d, c).wait_send()
-            w_y(d, c).wait_send()
+            for h in (0, 1):
+                w_x(d, c, h).wait_send()
+                w_y(d, c, h).wait_send()
         w_mate(d).wait_send()
     for k in range(1, 8):
         state_copy(k).wait_send()
@@ -411,7 +424,7 @@
     vmem = pl.BlockSpec(memory_space=pltpu.VMEM)
     return pl.pallas_call(
         kernel,
-        out_shape=jax.ShapeDtypeStruct((ROWS, WIDTH), BF16),
+        out_shape=pltpu.VMEM((ROWS, WIDTH), BF16),
         in_specs=[hbm] * 7,
         out_specs=vmem,
         scratch_shapes=[
@@ -433,9 +446,10 @@
             pltpu.VMEM((ROWS, WIDTH), BF16),
             pltpu.VMEM((2, ROWS, WIDTH), BF16),
             pltpu.VMEM((2, ROWS, WIDTH), BF16),
+            pltpu.VMEM((ROWS, WIDTH), F32),
             pltpu.VMEM((TILES, CHUNK, LANES), F32),
             dma((3,)), dma((3,)), dma((4,)), dma((4,)), dma((4,)),
-            dma((4, 2)), dma((4, 2)), dma((4, 2)), dma((4, 2)),
+            dma((4, 2, 2)), dma((4, 2, 2)), dma((4, 2, 2)), dma((4, 2, 2)),
             dma((8,)), dma((8,)),
             dma((CHUNKS,)), dma((CHUNKS,)), dma((CHUNKS,)), dma((CHUNKS,)),
             dma((CHUNKS,)), dma((CHUNKS,)),

time: 75.8 us -> 71.2 us (0.939)
  Pallas kernels: 73.4 us -> 70.1 us
  local copies, waits for them, and re-layouts: 2.26 us -> 0.97 us
    pallas_call x1, Pallas kernels: 73.4 us -> 70.1 us  [local(): pl.pallas_call(kernel, out_shape=pltpu.VMEM((ROWS, WIDTH), BF16), in_spec...]
    unnamed x1, local copies, waits for them, and re-layouts: 2.26 us -> 0.97 us
where the time goes in v4:
time: 71.2 us; the launch traced here: 71.1 us
  Pallas kernels  70.1 us (98%)
  local copies, waits for them, and re-layouts  0.97 us (1%)
    pallas_call x1, Pallas kernels, local(): pl.pallas_call(kernel, out_shape=pltpu.VMEM((ROWS, WIDTH), BF16), in_spec...  70.1 us

profile of v4, /device:TPU:1, one launch (start us, length us, event | category | flops | bytes accessed | tf_op | source)
XLA Modules:
  0.0 71.1 jit_solution(3581636309061131703)
XLA Ops:
  0.0 70.1 %layer.1 = bf16[1024,512]{1,0:T(8,128)(2,1)S(1)} custom-call(bf16[1024,512]{1,0:T(8,128)(2,1)} %q_hbm.1, bf16[1024,512]{1,0:T(8,128)(2,1)} %k_hbm.1, bf16[1024,512]{1,0:T(8,128)(2,1)} %v_hbm.1, f32[16,512]{1,0:T(8,128)} %horizon_hbm.1, f32[16,512]{1,0:T(8,128)} %residue_hbm.1, f32[1,512]{1,0:T(1,128)} %bitcast.1, bf16[512,8192]{1,0:T(8,128)(2,1)} %w_hbm.1), custom_call_target="tpu_custom_call" | custom-call | flops 8589934592 | bytes 13631488 | tf_op jit(solution)/shard_map/layer/pallas_call | solution.py:425
  70.1 1.0 %copy.9 = bf16[1024,512]{1,0:T(8,128)(2,1)} copy(bf16[1024,512]{1,0:T(8,128)(2,1)S(1)} %layer.1) | data formatting | bytes 2097152

commit v5 on v4

--- a/solution.py
+++ b/solution.py
@@ -115,15 +115,6 @@
         return pltpu.make_async_copy(
             w_hbm.at[:, columns(xl, d, core)], wn.at[d, pl.ds(0, WIDTH)], wl.at[d]
         )
-
-    pl.semaphore_wait(barrier, len(peers))
-    for c in (0, 1):
-        for h in (0, 1):
-            w_x(2, c, h).start()
-    for d in ORDER:
-        w_mate(d).start()
-    for d in ORDER:
-        w_own(d).start()
 
     for load in small:
         load.wait()
@@ -145,6 +136,15 @@
             coef[t, rows, :] = jnp.broadcast_to(scaled[m:m + 1, lane], (SUB, LANES))
         skips[t, :, :] = jnp.broadcast_to(skip_ref[:, lane], (SUB, LANES))
 
+    pl.semaphore_wait(barrier, len(peers))
+    for c in (0, 1):
+        for h in (0, 1):
+            w_x(2, c, h).start()
+    for d in ORDER:
+        w_mate(d).start()
+    for d in ORDER:
+        w_own(d).start()
+
     loads[0].wait()
     loads[1].wait()
     for t in range(TILES):
@@ -188,7 +188,13 @@
         return remote(ends.at[0], ends.at[k], st_s.at[k], st_r.at[k], later(k))
 
     for k in range(1, 8):
-        state_copy(k).start()
+        @pl.when(seq + k < 8)
+        def _(k=k):
+            state_copy(k).start()
+
+        @pl.when(k > seq)
+        def _(k=k):
+            ends[k, :, :] = jnp.zeros((MODES, WIDTH), F32)
     for d, c in ((1, 0), (1, 1), (3, 0), (3, 1), (0, 0), (0, 1)):
         for h in (0, 1):
             w_x(d, c, h).start()
@@ -206,10 +212,12 @@
             w_x(d, c, h).wait_recv()
             w_y(d, c, h).start()
 
-    for k in range(1, 8):
-        state_copy(k).wait_recv()
     pass_on(2, 0)
     pass_on(2, 1)
+    for k in range(1, 8):
+        @pl.when(k <= seq)
+        def _(k=k):
+            state_copy(k).wait_recv()
     incoming = jnp.zeros((MODES, WIDTH), F32)
     for k in range(7, 0, -1):
         incoming = jnp.where(k <= seq, device_decay * incoming + ends[k], incoming)
@@ -404,7 +412,9 @@
                 w_y(d, c, h).wait_send()
         w_mate(d).wait_send()
     for k in range(1, 8):
-        state_copy(k).wait_send()
+        @pl.when(seq + k < 8)
+        def _(k=k):
+            state_copy(k).wait_send()
 
     def finish(r, carry):
         g_x(r).wait_send()

time: 71.2 us -> 69.8 us (0.980)
  Pallas kernels: 70.1 us -> 68.7 us
    pallas_call x1, Pallas kernels: 70.1 us -> 68.7 us  [local(): pl.pallas_call(kernel, out_shape=pltpu.VMEM((ROWS, WIDTH), BF16), in_spec...]
where the time goes in v5:
time: 69.8 us; the launch traced here: 69.7 us
  Pallas kernels  68.7 us (98%)
  local copies, waits for them, and re-layouts  0.97 us (1%)
    pallas_call x1, Pallas kernels, local(): pl.pallas_call(kernel, out_shape=pltpu.VMEM((ROWS, WIDTH), BF16), in_spec...  68.7 us

profile of v5, /device:TPU:1, one launch (start us, length us, event | category | flops | bytes accessed | tf_op | source)
XLA Modules:
  0.0 69.7 jit_solution(9979181495477842974)
XLA Ops:
  0.0 68.7 %layer.1 = bf16[1024,512]{1,0:T(8,128)(2,1)S(1)} custom-call(bf16[1024,512]{1,0:T(8,128)(2,1)} %q_hbm.1, bf16[1024,512]{1,0:T(8,128)(2,1)} %k_hbm.1, bf16[1024,512]{1,0:T(8,128)(2,1)} %v_hbm.1, f32[16,512]{1,0:T(8,128)} %horizon_hbm.1, f32[16,512]{1,0:T(8,128)} %residue_hbm.1, f32[1,512]{1,0:T(1,128)} %bitcast.1, bf16[512,8192]{1,0:T(8,128)(2,1)} %w_hbm.1), custom_call_target="tpu_custom_call" | custom-call | flops 8589934592 | bytes 13631488 | tf_op jit(solution)/shard_map/layer/pallas_call | solution.py:435
  68.7 1.0 %copy.9 = bf16[1024,512]{1,0:T(8,128)(2,1)} copy(bf16[1024,512]{1,0:T(8,128)(2,1)S(1)} %layer.1) | data formatting | bytes 2097152
